TPU v7x, 32 devices: a whole 2x2x4 slice. The times are simulated.
32 devices in a mesh: ens: 2 (over x), lon: 4 (over y, core), lat: 4 (over z).
Axes of the slice: x: 2, y: 2, z: 4, core: 2. Of those that a mesh axis runs over, the one named last changes fastest.
Arguments:
- fields: bfloat16 [8, 768, 1024], P(('ens', 'lat'), 'lon'), parts along dimension 0, may hold values from -6 to 6
- conv_weight: bfloat16 [9216, 1024], P(None, 'lon'), may hold values from -0.0625 to 0.0625
- norm_gain: float32 [1024], replicated, may hold values from 0.1 to 1.9
- qkv_weight: bfloat16 [1024, 3072], replicated, may hold values from -0.1875 to 0.1875
- out_weight: bfloat16 [1024, 1024], replicated, may hold values from -0.1875 to 0.1875
- key_bias: bfloat16 [4, 768, 16], P('lat', 'lon'), may hold values from -8 to 250
Outputs:
- mixed: bfloat16 [8, 768, 1024], P(('ens', 'lat'), 'lon'), parts along dimension 0
There are 2 independent parts, one for each index of `ens`. A program takes and returns all parts, laid end to end along the dimension named above; an argument that names none is the same for every part. Nothing has to cross between parts.
All inputs are finite; a program needn't handle non-finite values.
Results may differ from a plain program's by a relative error of at most 0.012.
Values may be sent and summed in bfloat16 or wider, within the bound.
A program may use at most 128 MiB of HBM per device.

v0:
```python
import math

import jax
import jax.numpy as jnp
from jax import lax
from jax.sharding import PartitionSpec as P

H = 16


def extended(block, sides, width):
    for axis, dim in sides:
        count = lax.axis_size(axis)
        forward = [(i, i + 1) for i in range(count - 1)]
        backward = [(target, source) for source, target in forward]
        low = lax.ppermute(
            lax.slice_in_dim(block, block.shape[dim] - width, None, axis=dim), axis, forward
        )
        high = lax.ppermute(lax.slice_in_dim(block, 0, width, axis=dim), axis, backward)
        block = jnp.concatenate([low, block, high], axis=dim)
    return block


def tap_sum(wrapped, conv_weight, out_rows, lon_total, channels):
    out_width = conv_weight.shape[1]
    accum_cols = jnp.zeros((out_rows * lon_total, out_width), jnp.float32)
    tap_idx = 0
    for step_lat in (-1, 0, 1):
        for step_lon in (-1, 0, 1):
            shifted = wrapped[
                1 + step_lat : 1 + step_lat + out_rows, 1 + step_lon : 1 + step_lon + lon_total
            ].reshape(out_rows * lon_total, channels)
            accum_cols = accum_cols + jnp.dot(
                shifted,
                conv_weight[tap_idx * channels : (tap_idx + 1) * channels],
                preferred_element_type=jnp.float32,
            )
            tap_idx += 1
    return accum_cols.reshape(out_rows, lon_total, out_width)


def on_device(fields, conv_weight, norm_gain, qkv_weight, out_weight, key_bias):
    lat_n, lon_n, channels = fields.shape
    row_count = lat_n * lon_n
    head_dim = channels // H
    score_scale = 1.0 / math.sqrt(head_dim)
    banded = extended(fields, (("lat", 0),), 1)
    circle = lax.all_gather(banded, "lon", axis=1, tiled=True)
    lon_total = circle.shape[1]
    wrapped = jnp.concatenate([circle[:, -1:], circle, circle[:, :1]], axis=1)
    out_cols = tap_sum(wrapped, conv_weight, lat_n, lon_total, channels).astype(jnp.bfloat16)
    conv_out = lax.all_to_all(out_cols, "lon", split_axis=1, concat_axis=2, tiled=True).reshape(
        row_count, channels
    )
    residual = (
        fields.reshape(row_count, channels).astype(jnp.float32) + conv_out.astype(jnp.float32)
    ).astype(jnp.bfloat16)
    stream = residual.astype(jnp.float32)
    normed = (
        stream * lax.rsqrt(jnp.mean(stream * stream, axis=-1, keepdims=True) + 1e-06) * norm_gain
    ).astype(jnp.bfloat16)
    projected = jnp.dot(normed, qkv_weight, preferred_element_type=jnp.float32).astype(jnp.bfloat16)
    queries = projected[:, :channels].reshape(lat_n, lon_n, channels)
    key_rows = projected[:, channels : 2 * channels].reshape(lat_n, lon_n, channels)
    value_rows = projected[:, 2 * channels :].reshape(lat_n, lon_n, channels)
    query_heads = queries.reshape(lat_n, lon_n, H, head_dim)
    best = jnp.full((lat_n, H, lon_n), -1e30, jnp.float32)
    key_part = lax.all_gather(key_rows, "lon", axis=1, tiled=True)
    value_part = lax.all_gather(value_rows, "lon", axis=1, tiled=True)
    bias_part = lax.all_gather(key_bias, "lon", axis=1, tiled=True)
    span = key_part.shape[1]
    key_heads = key_part.reshape(lat_n, span, H, head_dim)
    value_heads = value_part.reshape(lat_n, span, H, head_dim)
    scores = (
        jnp.einsum("aqhd,akhd->ahqk", query_heads, key_heads, preferred_element_type=jnp.float32)
        * score_scale
    )
    scores = scores + jnp.transpose(bias_part, (0, 2, 1)).astype(jnp.float32)[:, :, None, :]
    new_best = jnp.maximum(best, jnp.max(scores, axis=-1))
    weights = jnp.exp(scores - new_best[..., None])
    denom = jnp.sum(weights, axis=-1)
    accum = jnp.einsum(
        "ahqk,akhd->ahqd",
        weights.astype(jnp.bfloat16),
        value_heads,
        preferred_element_type=jnp.float32,
    )
    best, denom, accum = (new_best, denom, accum)
    attended = (
        jnp.transpose(accum / denom[..., None], (0, 2, 1, 3))
        .reshape(row_count, channels)
        .astype(jnp.bfloat16)
    )
    mixed = residual.astype(jnp.float32) + jnp.dot(
        attended, out_weight, preferred_element_type=jnp.float32
    )
    return mixed.astype(jnp.bfloat16).reshape(lat_n, lon_n, channels)


def solution(mesh):
    return jax.shard_map(
        on_device,
        mesh=mesh,
        in_specs=(
            P(("ens", "lat"), "lon", None),
            P(None, "lon"),
            P(),
            P(),
            P(),
            P("lat", "lon", None),
        ),
        out_specs=P(("ens", "lat"), "lon", None),
        check_vma=False,
    )
```

profile of v0, /device:TPU:0, one launch (start us, length us, event | category | flops | bytes accessed | tf_op | source)
XLA Modules:
  0.0 157.3 jit_solution(3155669633497849721)
XLA Ops:
  6.5 5.1 %collective-permute-start = (bf16[1,192,1024]{2,1,0:T(8,128)(2,1)}, bf16[1,192,1024]{2,1,0:T(8,128)(2,1)S(1)}, u32[]{:S(2)}, u32[]{:S(2)}) collective-permute-start(bf16[1,192,1024]{2,1,0:T(8,128)(2,1)} %param.6), channel_id=1, source_target_pairs={{0,1},{1,2},{2,3},{4,5},{5,6},{6,7},{8,9},{9,10},{10,11},{12,13},{... | collective-permute-start | bytes 1179656 | tf_op jit(solution)/shard_map/ppermute | solution.py:16
  11.6 1.3 collective-permute-start.1
  12.9 7.3 %collective-permute-done = bf16[1,192,1024]{2,1,0:T(8,128)(2,1)S(1)} collective-permute-done((bf16[1,192,1024]{2,1,0:T(8,128)(2,1)}, bf16[1,192,1024]{2,1,0:T(8,128)(2,1)S(1)}, u32[]{:S(2)}, u32[]{:S(2)}) %collective-permute-start) | collective-permute-done | bytes 393248 | tf_op jit(solution)/shard_map/ppermute | solution.py:16
  20.3 4.0 %collective-permute-done.1 = bf16[1,192,1024]{2,1,0:T(8,128)(2,1)S(1)} collective-permute-done((bf16[1,192,1024]{2,1,0:T(8,128)(2,1)}, bf16[1,192,1024]{2,1,0:T(8,128)(2,1)S(1)}, u32[]{:S(2)}, u32[]{:S(2)}) %collective-permute-start.1) | collective-permute-done | bytes 393248 | tf_op jit(solution)/shard_map/ppermute | solution.py:19
  24.3 2.2 %pad_maximum_fusion.2 = bf16[3,192,1024]{2,1,0:T(8,128)(2,1)} fusion(bf16[1,192,1024]{2,1,0:T(8,128)(2,1)S(1)} %collective-permute-done.1, bf16[1,192,1024]{2,1,0:T(8,128)(2,1)} %param.6, bf16[1,192,1024]{2,1,0:T(8,128)(2,1)S(1)} %collective-permute-done), kind=kLoop, calls=%fused_computation.52 | loop fusion | flops 1179648 | bytes 2359296 | tf_op jit(solution)/shard_map/concatenate | solution.py:20
  26.6 37.8 %all-gather.6.cloned.1.call-done = bf16[3,768,1024]{2,1,0:T(8,128)(2,1)} async-done(((bf16[3,192,1024]{2,1,0:T(8,128)(2,1)}), bf16[3,768,1024]{2,1,0:T(8,128)(2,1)}) %all-gather.6.cloned.1.call-update) | async-done | bytes 4718608 | tf_op jit(solution)/shard_map/all_gather | solution.py:48
  64.4 1.0 fusion.66
  65.4 2.3 %fusion.14 = f32[768,256]{1,0:T(8,128)S(1)} fusion(bf16[3,1,1024]{2,1,0:T(2,128)(2,1)S(1)} %get-tuple-element.8, bf16[3,768,1024]{2,1,0:T(8,128)(2,1)} %all-gather.6.cloned.1.call-done, bf16[9216,256]{1,0:T(8,128)(2,1)} %param.7), kind=kOutput, calls=%fused_computation.18 | convolution fusion | flops 405798912 | bytes 6035456 | tf_op jit(solution)/shard_map/dot_general | solution.py:33
  67.7 1.8 %fusion.21 = f32[768,256]{1,0:T(8,128)S(1)} fusion(bf16[3,1,1024]{2,1,0:T(2,128)(2,1)S(1)} %get-tuple-element.8, bf16[3,768,1024]{2,1,0:T(8,128)(2,1)S(1)} %copy-done.1, bf16[9216,256]{1,0:T(8,128)(2,1)} %param.7), kind=kOutput, calls=%fused_computation.28 | convolution fusion | flops 405798912 | bytes 6035456 | tf_op jit(solution)/shard_map/dot_general | solution.py:33
  69.5 0.7 copy-done.3
  71.4 0.6 fusion.6
  72.0 0.6 fusion.17
  73.1 0.6 fusion.9
  73.7 0.8 fusion.39
  74.5 0.6 copy.24
  75.7 3.7 %reduce.4 = bf16[768,256]{1,0:T(8,128)(2,1)} reduce(bf16[768,1,256]{2,1,0:T(2,128)(2,1)S(1)} %bitcast.83, bf16[]{:T(256)} %broadcast.26), dimensions={1}, to_apply=%bitcast.81.reduce_sub_computation | reduce | bytes 786434
  79.4 1.1 reshape.124
  80.5 10.5 %all_to_all.4 = bf16[4,2,24576]{2,1,0:T(2,128)(2,1)} all-to-all(bf16[4,2,24576]{2,1,0:T(2,128)(2,1)S(1)} %reshape.124), channel_id=1, replica_groups=mesh['ens'=2,'lon'=4,'lat'=4] {'lon'}, dimensions={0} | all-to-all | bytes 786432 | tf_op jit(solution)/shard_map/all_to_all | solution.py:52
  91.1 2.1 %reshape.125 = bf16[768,1,256]{2,1,0:T(2,128)(2,1)S(1)} reshape(bf16[4,2,24576]{2,1,0:T(2,128)(2,1)} %all_to_all.4) | data formatting | bytes 786432
  94.1 4.3 %convolution_convert_fusion = bf16[192,3072]{1,0:T(8,128)(2,1)S(1)} fusion(bf16[1024,3072]{1,0:T(8,128)(2,1)} %param.9, bf16[192,1024]{1,0:T(8,128)(2,1)S(1)} %get-tuple-element.6, f32[1024]{0:T(1024)S(1)} %copy-done.6, f32[192]{0:T(256)S(1)} %add_rsqrt_fusion), kind=kOutput, calls=%fused_computation.6 | convolution fusion | flops 1209335808 | bytes 7869184 | tf_op jit(solution)/shard_map/dot_general | solution.py:62
  98.4 1.0 fusion.67
  99.4 0.7 all-gather.10.cloned.1.call-update
  100.2 6.3 %all_gather.14 = bf16[1,768,16]{2,0,1:T(2,128)(2,1)S(1)} all-gather(bf16[1,192,16]{2,0,1:T(2,128)(2,1)S(1)} %copy.19), channel_id=1, replica_groups=mesh['ens'=2,'lon'=4,'lat'=4] {'lon'}, dimensions={1}, use_global_device_ids=true | all-gather | bytes 30720 | tf_op jit(solution)/shard_map/all_gather | solution.py:70
  107.3 11.9 %all-gather.8.cloned.1.call-done = bf16[768,1024]{1,0:T(8,128)(2,1)} async-done(((bf16[192,1024]{1,0:T(8,128)(2,1)}), bf16[768,1024]{1,0:T(8,128)(2,1)}) %all-gather.8.cloned.1.call-update) | async-done | bytes 1572880 | tf_op jit(solution)/shard_map/all_gather | solution.py:68
  119.2 2.6 %copy.18 = bf16[768,1024]{0,1:T(8,128)(2,1)} copy(bf16[768,1024]{1,0:T(8,128)(2,1)} %all-gather.8.cloned.1.call-done) | data formatting | bytes 3145728 | tf_op jit(solution)/shard_map/all_gather | solution.py:68
  121.8 3.0 %fusion = (f32[16,192]{1,0:T(8,128)S(1)}, f32[16,192,768]{2,1,0:T(8,128)S(1)}) fusion(f32[16,768]{1,0:T(8,128)S(1)} %copy.20, bf16[192,16,64]{0,2,1:T(8,128)(2,1)S(1)} %bitcast.87, bf16[768,16,64]{0,2,1:T(8,128)(2,1)} %bitcast.82), kind=kOutput, calls=%fused_computation.2 | convolution fusion | flops 309064704 | bytes 11464704 | tf_op jit(solution)/shard_map/aqhd,akhd->ahqk/dot_general | solution.py:75
  124.8 3.6 %copy-done.2 = f32[16,192,768]{2,1,0:T(8,128)} copy-done((f32[16,192,768]{2,1,0:T(8,128)}, f32[16,192,768]{2,1,0:T(8,128)S(1)}, u32[]{:S(2)}) %copy-start.2) | copy-done | bytes 9437208
  128.4 2.4 %fusion.1 = f32[16,192]{1,0:T(8,128)S(1)} fusion(f32[16,192,768]{2,1,0:T(8,128)S(1)} %get-tuple-element.13, f32[16,192]{1,0:T(8,128)S(1)} %broadcast_maximum_fusion, f32[16,768]{1,0:T(8,128)S(1)} %copy.20), kind=kLoop, calls=%fused_computation.3 | loop fusion | flops 9434112 | bytes 9510912 | tf_op jit(solution)/shard_map/reduce_sum | solution.py:81
  130.8 9.6 %all-gather.10.cloned.1.call-done = bf16[768,1024]{1,0:T(8,128)(2,1)} async-done(((bf16[192,1024]{1,0:T(8,128)(2,1)}), bf16[768,1024]{1,0:T(8,128)(2,1)}) %all-gather.10.cloned.1.call-update) | async-done | bytes 1572880 | tf_op jit(solution)/shard_map/all_gather | solution.py:69
  140.4 2.6 %copy.21 = bf16[768,1024]{0,1:T(8,128)(2,1)} copy(bf16[768,1024]{1,0:T(8,128)(2,1)} %all-gather.10.cloned.1.call-done) | data formatting | bytes 3145728 | tf_op jit(solution)/shard_map/all_gather | solution.py:69
  143.0 6.4 %divide_convert_fusion = bf16[16,192,64]{1,2,0:T(8,128)(2,1)S(1)} fusion(bf16[768,16,64]{0,2,1:T(8,128)(2,1)} %bitcast.88, f32[16,192,768]{2,1,0:T(8,128)} %copy-done.2, f32[16,192]{1,0:T(8,128)S(1)} %broadcast_maximum_fusion, f32[16,768]{1,0:T(8,128)S(1)} %copy.20, f32[16,192]{1,0:T(8,128)S(1)} %fusion.1), kind=kOutput, calls=%fused_computation.53 | convolution fusion | flops 311820288 | bytes 11476992 | tf_op jit(solution)/shard_map/ahqk,akhd->ahqd/dot_general | solution.py:82
  149.4 1.3 fusion.38
  (30 shorter events, 4.2 us)
Async XLA Ops:
  6.5 142.9 %copy-start = (bf16[1024,1024]{1,0:T(8,128)(2,1)S(1)}, bf16[1024,1024]{1,0:T(8,128)(2,1)}, u32[]{:S(2)}) copy-start(bf16[1024,1024]{1,0:T(8,128)(2,1)} %param.10) | copy-start | bytes 6291460
  6.5 57.8 %all-gather.6.cloned.1.call-start = ((), (), s32[]{:S(2)}) async-start(), calls=%async_computation.1 | async-start | bytes 5898240 | tf_op jit(solution)/shard_map/all_gather | solution.py:48
  6.5 13.7 %collective-permute-start = (bf16[1,192,1024]{2,1,0:T(8,128)(2,1)}, bf16[1,192,1024]{2,1,0:T(8,128)(2,1)S(1)}, u32[]{:S(2)}, u32[]{:S(2)}) collective-permute-start(bf16[1,192,1024]{2,1,0:T(8,128)(2,1)} %param.6), channel_id=1, source_target_pairs={{0,1},{1,2},{2,3},{4,5},{5,6},{6,7},{8,9},{9,10},{10,11},{12,13},{... | collective-permute-start | bytes 1179656 | tf_op jit(solution)/shard_map/ppermute | solution.py:16
  11.6 12.7 %collective-permute-start.1 = (bf16[1,192,1024]{2,1,0:T(8,128)(2,1)}, bf16[1,192,1024]{2,1,0:T(8,128)(2,1)S(1)}, u32[]{:S(2)}, u32[]{:S(2)}) collective-permute-start(bf16[1,192,1024]{2,1,0:T(8,128)(2,1)} %param.6), channel_id=1, source_target_pairs={{1,0},{2,1},{3,2},{5,4},{6,5},{7,6},{9,8},{10,9},{11,10},{13,12},{... | collective-permute-start | bytes 1179656 | tf_op jit(solution)/shard_map/ppermute | solution.py:19
  26.5 92.6 %all-gather.8.cloned.1.call-start = ((), (), s32[]{:S(2)}) async-start(), calls=%async_computation.2 | async-start | bytes 1966080 | tf_op jit(solution)/shard_map/all_gather | solution.py:68
  64.4 3.4 %copy-start.1 = (bf16[3,768,1024]{2,1,0:T(8,128)(2,1)S(1)}, bf16[3,768,1024]{2,1,0:T(8,128)(2,1)}, u32[]{:S(2)}) copy-start(bf16[3,768,1024]{2,1,0:T(8,128)(2,1)} %all-gather.6.cloned.1.call-done) | copy-start | bytes 14155780
  67.7 2.5 %copy-start.3 = (bf16[9216,256]{1,0:T(8,128)(2,1)S(1)}, bf16[9216,256]{1,0:T(8,128)(2,1)}, u32[]{:S(2)}) copy-start(bf16[9216,256]{1,0:T(8,128)(2,1)} %param.7) | copy-start | bytes 14155780
  79.4 14.5 %copy-start.4 = (bf16[1,192,1024]{2,1,0:T(8,128)(2,1)S(1)}, bf16[1,192,1024]{2,1,0:T(8,128)(2,1)}, u32[]{:S(2)}) copy-start(bf16[1,192,1024]{2,1,0:T(8,128)(2,1)} %param.6) | copy-start | bytes 1179652
  91.1 3.0 %copy-start.6 = (f32[1024]{0:T(1024)S(1)}, f32[1024]{0:T(1024)}, u32[]{:S(2)}) copy-start(f32[1024]{0:T(1024)} %param.8) | copy-start | bytes 12292
  98.3 1.7 %copy-start.5 = (bf16[1,192,16]{1,2,0:T(8,128)(2,1)S(1)}, bf16[1,192,16]{1,2,0:T(8,128)(2,1)}, u32[]{:S(2)}) copy-start(bf16[1,192,16]{1,2,0:T(8,128)(2,1)} %param.11) | copy-start | bytes 18436
  99.3 41.1 %all-gather.10.cloned.1.call-start = ((), (), s32[]{:S(2)}) async-start(), calls=%async_computation.3 | async-start | bytes 1966080 | tf_op jit(solution)/shard_map/all_gather | solution.py:69
  124.7 3.7 %copy-start.2 = (f32[16,192,768]{2,1,0:T(8,128)}, f32[16,192,768]{2,1,0:T(8,128)S(1)}, u32[]{:S(2)}) copy-start(f32[16,192,768]{2,1,0:T(8,128)S(1)} %get-tuple-element.13) | copy-start | bytes 28311556
Sparse Core Ops, SparseCore 0:
  26.6 37.6 all-gather.5
  99.5 19.6 all-gather.7
  120.7 19.6 all-gather.9
where the time goes:
time: 158 us; the launch traced here: 157 us
  waiting for transfers between devices  71.4 us (45%)
  matrix products  23.3 us (15%)
  local copies, waits for them, and re-layouts  17 us (11%)
  blocking collectives  16.8 us (11%)
  between operations  13.3 us (8%)
  other arithmetic  8.93 us (6%)
  starting transfers between devices  6.45 us (4%)
    all_gather x1, waiting for transfers between devices, on_device(): circle = lax.all_gather(banded, 'lon', axis=1, tiled=True)  37.8 us
    all_gather x1, waiting for transfers between devices, on_device(): key_part = lax.all_gather(key_rows, 'lon', axis=1, tiled=True)  11.9 us
    all_to_all x1, blocking collectives, on_device(): lax.all_to_all(out_cols, 'lon', split_axis=1, concat_axis=2, tiled=True)  10.5 us
    all_gather x1, waiting for transfers between devices, on_device(): value_part = lax.all_gather(value_rows, 'lon', axis=1, tiled=True)  9.63 us
    unnamed x19, local copies, waits for them, and re-layouts  8.43 us
    dot_general x9, matrix products, tap_sum(): jnp.dot(shifted, conv_weight[tap_idx * channels:(tap_idx + 1) * channels]...  8.34 us
    ppermute x1, waiting for transfers between devices, extended(): lax.ppermute(lax.slice_in_dim(block, block.shape[dim] - width, None, axis...  7.35 us
    dot_general x1, matrix products, on_device(): jnp.einsum('ahqk,akhd->ahqd', weights.astype(jnp.bfloat16), value_heads,...  6.37 us
  transfers between devices with their start and end apart: 5, of which 5 were waited for; matrix products, arithmetic and copies ran while one was open for 6% of the time, Pallas kernels for 0%

commit v1 on v0

--- a/solution.py
+++ b/solution.py
@@ -1,8 +1,11 @@
+import functools
 import math
 
 import jax
 import jax.numpy as jnp
 from jax import lax
+from jax.experimental import pallas as pl
+from jax.experimental.pallas import tpu as pltpu
 from jax.sharding import PartitionSpec as P
 
 H = 16
@@ -97,9 +100,382 @@
     return mixed.astype(jnp.bfloat16).reshape(lat_n, lon_n, channels)
 
 
+MESH = pl.DeviceIdType.MESH
+EDGE = 16
+PIECES = 2
+OWN_SIB, EDGE_P, EDGE_Q, BIAS_SIB, BIAS_P, BIAS_Q = 0, 1, 2, 3, 4, 5
+CONV_P, CONV_SIB, CONV_FWD = 6, 8, 10
+UP, DOWN = 12, 14
+ATT_P, ATT_Q, ATT_SIB = 16, 17, 18
+PIECE, PIECE_FWD = 19, 19 + PIECES
+COPIES = 19 + 2 * PIECES
+
+
+def block_kernel(
+    lat_count,
+    fields_ref,
+    conv_ref,
+    gain_ref,
+    qkv_ref,
+    outw_ref,
+    bias_ref,
+    out_ref,
+    xbuf,
+    conv_w,
+    qkv_w,
+    out_w,
+    bias_own,
+    bias_all,
+    part_send,
+    part_recv,
+    centre,
+    cols,
+    resid,
+    normed,
+    proj,
+    att_send,
+    att,
+    send_sem,
+    recv_sem,
+    load_sem,
+):
+    n, channels = fields_ref.shape[1], fields_ref.shape[2]
+    width = conv_ref.shape[1]
+    half = 2 * n
+    blocks = channels // width
+    head_dim = channels // H
+    me, row = lax.axis_index("lon"), lax.axis_index("lat")
+    y, c = me // 2, me % 2
+    sib, p, q = 2 * y + 1 - c, 2 * (1 - y) + c, 2 * (1 - y) + 1 - c
+    above, below = row > 0, row < lat_count - 1
+
+    def load(src, dst, idx):
+        copy = pltpu.make_async_copy(src, dst, load_sem.at[idx])
+        copy.start()
+        return copy
+
+    def remote(src, dst, idx, target):
+        return pltpu.make_async_remote_copy(
+            src_ref=src,
+            dst_ref=dst,
+            send_sem=send_sem.at[idx],
+            recv_sem=recv_sem.at[idx],
+            device_id=target,
+            device_id_type=MESH,
+        )
+
+    def rows_at(offset, count):
+        return pl.ds(pl.multiple_of(offset, EDGE), count)
+
+    own = fields_ref.at[0]
+    loads = [load(own, xbuf.at[0, rows_at(EDGE + c * n, n)], 0)]
+    tap_rows = 3 * channels
+    for idx, a in ((1, 2), (2, 0), (3, 1)):
+        span = pl.ds(a * tap_rows, tap_rows)
+        loads.append(load(conv_ref.at[span], conv_w.at[span], idx))
+    for j in range(3):
+        lanes = pl.ds(pl.multiple_of(j * channels + me * width, width), width)
+        loads.append(load(qkv_ref.at[:, lanes], qkv_w.at[j], 4 + j))
+    loads.append(load(outw_ref, out_w, 7))
+
+    barrier = pltpu.get_barrier_semaphore()
+    for other in (sib, p, q):
+        pl.semaphore_signal(barrier, inc=1, device_id={"lon": other}, device_id_type=MESH)
+
+    @pl.when(above)
+    def _():
+        pl.semaphore_signal(barrier, inc=1, device_id={"lat": row - 1}, device_id_type=MESH)
+
+    @pl.when(below)
+    def _():
+        pl.semaphore_signal(barrier, inc=1, device_id={"lat": row + 1}, device_id_type=MESH)
+
+    lane = lax.broadcasted_iota(jnp.int32, (H, 2 * head_dim), 1)
+    which = lax.broadcasted_iota(jnp.int32, (H, 2 * head_dim), 0)
+    spread = jnp.where((lane == which) | (lane == which + head_dim), 1.0, 0.0).astype(jnp.bfloat16)
+    bias_own[...] = jnp.dot(bias_ref[0], spread, preferred_element_type=jnp.float32).astype(
+        jnp.bfloat16
+    )
+    bias_all[rows_at(c * n, n)] = bias_own[...]
+
+    pl.semaphore_wait(barrier, 3 + above.astype(jnp.int32) + below.astype(jnp.int32))
+
+    sends = []
+
+    def begin(copy):
+        copy.start()
+        sends.append(copy)
+        return copy
+
+    edge_src = fields_ref.at[0, rows_at(c * (n - EDGE), EDGE)]
+    edge_dst = xbuf.at[0, rows_at((1 - c) * (EDGE + half), EDGE)]
+    edges = [
+        begin(remote(edge_src, edge_dst, EDGE_P, {"lon": p})),
+        begin(remote(edge_src, edge_dst, EDGE_Q, {"lon": q})),
+    ]
+    to_sib = begin(
+        remote(own, xbuf.at[0, rows_at(EDGE + c * n, n)], OWN_SIB, {"lon": sib})
+    )
+    piece = n // PIECES
+    pieces = [
+        begin(
+            remote(
+                fields_ref.at[0, pl.ds(g * piece, piece)],
+                xbuf.at[1, rows_at(EDGE + c * n + g * piece, piece)],
+                PIECE + g,
+                {"lon": p},
+            )
+        )
+        for g in range(PIECES)
+    ]
+    biases = [
+        begin(remote(bias_own, bias_all.at[rows_at(c * n, n)], BIAS_SIB, {"lon": sib})),
+        begin(remote(bias_own, bias_all.at[rows_at(half + c * n, n)], BIAS_P, {"lon": p})),
+        begin(remote(bias_own, bias_all.at[rows_at(half + c * n, n)], BIAS_Q, {"lon": q})),
+    ]
+
+    def taps(k, a):
+        full = EDGE + half + EDGE
+        total = None
+        for b in range(3):
+            tap = 3 * a + b
+            part = jnp.dot(
+                xbuf[k],
+                conv_w[tap * channels : (tap + 1) * channels],
+                preferred_element_type=jnp.float32,
+            )
+            if b != 1:
+                part = pltpu.roll(part, (1 - b) % full, 0)
+            total = part if total is None else total + part
+        return total[EDGE : EDGE + half]
+
+    up = [
+        remote(part_send.at[k, 0], part_recv.at[k, 0], UP + k, {"lat": row - 1}) for k in range(2)
+    ]
+    down = [
+        remote(part_send.at[k, 1], part_recv.at[k, 1], DOWN + k, {"lat": row + 1})
+        for k in range(2)
+    ]
+
+    def send_up(k):
+        part_send[k, 0] = taps(k, 2).astype(jnp.bfloat16)
+        pl.when(above)(up[k].start)
+
+    def send_down(k):
+        part_send[k, 1] = taps(k, 0).astype(jnp.bfloat16)
+        pl.when(below)(down[k].start)
+
+    conv_p = [
+        remote(cols.at[k, me], cols.at[1 - k, me], CONV_P + k, {"lon": p}) for k in range(2)
+    ]
+    conv_sib = [
+        remote(cols.at[k, me], cols.at[k, me], CONV_SIB + k, {"lon": sib}) for k in range(2)
+    ]
+    conv_fwd = [
+        remote(cols.at[1 - k, p], cols.at[1 - k, p], CONV_FWD + k, {"lon": sib})
+        for k in range(2)
+    ]
+
+    def finish_conv(k):
+        @pl.when(below)
+        def _():
+            up[k].wait_recv()
+            centre[k] = centre[k] + part_recv[k, 0].astype(jnp.float32)
+
+        @pl.when(above)
+        def _():
+            down[k].wait_recv()
+            centre[k] = centre[k] + part_recv[k, 1].astype(jnp.float32)
+
+        cols[k, me] = centre[k].astype(jnp.bfloat16)
+        begin(conv_p[k])
+        begin(conv_sib[k])
+
+    loads[0].wait()
+    to_sib.wait_recv()
+    for copy in edges:
+        copy.wait_recv()
+    xbuf[1, 0:EDGE] = xbuf[0, half : half + EDGE]
+    xbuf[1, EDGE + half : EDGE + half + EDGE] = xbuf[0, EDGE : EDGE + EDGE]
+    loads[1].wait()
+    send_up(0)
+    loads[2].wait()
+    send_down(0)
+    loads[3].wait()
+    centre[0] = taps(0, 1)
+
+    forwards = []
+    for g in range(PIECES):
+        pieces[g].wait_recv()
+        got = xbuf.at[1, rows_at(EDGE + c * n + g * piece, piece)]
+        forwards.append(begin(remote(got, got, PIECE_FWD + g, {"lon": sib})))
+    finish_conv(0)
+    for copy in forwards:
+        copy.wait_recv()
+    send_up(1)
+    send_down(1)
+    centre[1] = taps(1, 1)
+    conv_p[0].wait_recv()
+    begin(conv_fwd[0])
+    finish_conv(1)
+
+    for j in range(3):
+        loads[4 + j].wait()
+
+    def project(k):
+        squares = jnp.zeros((half, 1), jnp.float32)
+        for o in range(blocks):
+            lanes = slice(o * width, (o + 1) * width)
+            summed = (
+                xbuf[k, EDGE : EDGE + half, lanes].astype(jnp.float32)
+                + cols[k, o].astype(jnp.float32)
+            ).astype(jnp.bfloat16)
+            resid[k, :, lanes] = summed
+            wide = summed.astype(jnp.float32)
+            squares = squares + jnp.sum(wide * wide, axis=-1, keepdims=True)
+        scale = lax.rsqrt(squares / channels + 1e-06)
+        for o in range(blocks):
+            lanes = slice(o * width, (o + 1) * width)
+            normed[:, lanes] = (
+                resid[k, :, lanes].astype(jnp.float32) * scale * gain_ref[:, lanes]
+            ).astype(jnp.bfloat16)
+        for j in range(3):
+            proj[j, k * half : (k + 1) * half] = jnp.dot(
+                normed[...], qkv_w[j], preferred_element_type=jnp.float32
+            ).astype(jnp.bfloat16)
+
+    conv_sib[1].wait_recv()
+    conv_fwd[0].wait_recv()
+    project(1)
+    conv_p[1].wait_recv()
+    begin(conv_fwd[1])
+    conv_sib[0].wait_recv()
+    conv_fwd[1].wait_recv()
+    project(0)
+    for copy in biases:
+        copy.wait_recv()
+
+    tile = 2 * head_dim
+    score_scale = 1.0 / math.sqrt(head_dim)
+    low_q = lax.broadcasted_iota(jnp.int32, (n, tile), 1)
+    low_k = lax.broadcasted_iota(jnp.int32, (2 * half, tile), 1)
+
+    def attend(offset, dst):
+        for pair in range(width // tile):
+            lanes = slice(pair * tile, (pair + 1) * tile)
+            queries = proj[0, rows_at(offset, n), lanes].astype(jnp.float32) * score_scale
+            keys, values = proj[1, :, lanes], proj[2, :, lanes]
+            outs = []
+            for odd in range(2):
+                head = me * (width // head_dim) + 2 * pair + odd
+                mine_q = (low_q >= head_dim) if odd else (low_q < head_dim)
+                mine_k = (low_k >= head_dim) if odd else (low_k < head_dim)
+                picked = jnp.where(low_q == head + (0 if odd else head_dim), 1.0, 0.0)
+                q_ext = jnp.where(mine_q, queries, picked).astype(jnp.bfloat16)
+                k_ext = jnp.where(mine_k, keys, bias_all[...])
+                scores = lax.dot_general(
+                    q_ext, k_ext, (((1,), (1,)), ((), ())), preferred_element_type=jnp.float32
+                )
+                weights = jnp.exp(scores - jnp.max(scores, axis=-1, keepdims=True))
+                total = jnp.sum(weights, axis=-1, keepdims=True)
+                summed = jnp.dot(
+                    weights.astype(jnp.bfloat16), values, preferred_element_type=jnp.float32
+                )
+                outs.append(summed / total)
+            dst[:, lanes] = jnp.where(low_q < head_dim, outs[0], outs[1]).astype(jnp.bfloat16)
+
+    attend(half + (1 - c) * n, att_send.at[0])
+    att_q = begin(remote(att_send.at[0], att.at[me], ATT_Q, {"lon": q}))
+    attend(half + c * n, att_send.at[1])
+    att_p = begin(remote(att_send.at[1], att.at[me], ATT_P, {"lon": p}))
+    attend((1 - c) * n, att_send.at[2])
+    att_s = begin(remote(att_send.at[2], att.at[me], ATT_SIB, {"lon": sib}))
+    attend(c * n, att.at[me])
+    loads[7].wait()
+    for copy in (att_s, att_q, att_p):
+        copy.wait_recv()
+
+    for j in range(blocks):
+        lanes = slice(j * width, (j + 1) * width)
+        mixed = resid[0, rows_at(c * n, n), lanes].astype(jnp.float32)
+        for o in range(blocks):
+            mixed = mixed + jnp.dot(
+                att[o], out_w[o * width : (o + 1) * width, lanes], preferred_element_type=jnp.float32
+            )
+        out_ref[0, :, lanes] = mixed.astype(jnp.bfloat16)
+
+    for copy in sends:
+        copy.wait_send()
+    for k in range(2):
+        pl.when(above)(up[k].wait_send)
+        pl.when(below)(down[k].wait_send)
+
+
+def fused(fields, conv_weight, norm_gain, qkv_weight, out_weight, key_bias):
+    _, n, channels = fields.shape
+    width = conv_weight.shape[1]
+    half = 2 * n
+    lat_count = lax.axis_size("lat")
+    lon_count = lax.axis_size("lon")
+    head_dim = channels // H
+    bf16, f32 = jnp.bfloat16, jnp.float32
+    any_spec = pl.BlockSpec(memory_space=pl.ANY)
+    vmem_spec = pl.BlockSpec(memory_space=pltpu.VMEM)
+    return pl.pallas_call(
+        functools.partial(block_kernel, lat_count),
+        out_shape=jax.ShapeDtypeStruct(fields.shape, bf16),
+        in_specs=[any_spec, any_spec, vmem_spec, any_spec, any_spec, vmem_spec],
+        out_specs=vmem_spec,
+        scratch_shapes=[
+            pltpu.VMEM((2, half + 2 * EDGE, channels), bf16),
+            pltpu.VMEM(conv_weight.shape, bf16),
+            pltpu.VMEM((3, channels, width), bf16),
+            pltpu.VMEM(out_weight.shape, bf16),
+            pltpu.VMEM((n, 2 * head_dim), bf16),
+            pltpu.VMEM((2 * half, 2 * head_dim), bf16),
+            pltpu.VMEM((2, 2, half, width), bf16),
+            pltpu.VMEM((2, 2, half, width), bf16),
+            pltpu.VMEM((2, half, width), f32),
+            pltpu.VMEM((2, lon_count, half, width), bf16),
+            pltpu.VMEM((2, half, channels), bf16),
+            pltpu.VMEM((half, channels), bf16),
+            pltpu.VMEM((3, 2 * half, width), bf16),
+            pltpu.VMEM((3, n, width), bf16),
+            pltpu.VMEM((lon_count, n, width), bf16),
+            pltpu.SemaphoreType.DMA((COPIES,)),
+            pltpu.SemaphoreType.DMA((COPIES,)),
+            pltpu.SemaphoreType.DMA((8,)),
+        ],
+        compiler_params=pltpu.CompilerParams(
+            collective_id=0, has_side_effects=True, vmem_limit_bytes=44 * 1024 * 1024
+        ),
+    )(fields, conv_weight, norm_gain.reshape(1, channels), qkv_weight, out_weight, key_bias)
+
+
+def suits_kernel(fields, conv_weight):
+    lat_n, n, channels = fields.shape
+    width = conv_weight.shape[1]
+    head_dim = channels // H
+    return (
+        lat_n == 1
+        and lax.axis_size("lon") == 4
+        and n % (EDGE * PIECES) == 0
+        and width % 128 == 0
+        and 2 * head_dim == 128
+        and H <= head_dim
+        and n * channels <= 2**18
+    )
+
+
+def per_device(fields, conv_weight, *others):
+    if suits_kernel(fields, conv_weight):
+        return fused(fields, conv_weight, *others)
+    return on_device(fields, conv_weight, *others)
+
+
 def solution(mesh):
     return jax.shard_map(
-        on_device,
+        per_device,
         mesh=mesh,
         in_specs=(
             P(("ens", "lat"), "lon", None),

time: 158 us -> 50.2 us (0.32)
  waiting for transfers between devices: 71.4 us -> 0 us
  Pallas kernels: 0 us -> 42.7 us
  matrix products: 23.3 us -> 0 us
  blocking collectives: 16.8 us -> 0 us
  between operations: 13.3 us -> 0.02 us
  local copies, waits for them, and re-layouts: 17 us -> 7.17 us
  other arithmetic: 8.93 us -> 0 us
  starting transfers between devices: 6.45 us -> 0 us
    all_gather x3 -> x0, waiting for transfers between devices: 59.3 us -> none  [the longest x1 37.8 us: on_device(): circle = lax.all_gather(banded, 'lon', axis=1, tiled=True)]
    pallas_call x0 -> x1, Pallas kernels: none -> 42.7 us  [fused(): pl.pallas_call(functools.partial(block_kernel, lat_count), out_shape=jax....]
    dot_general x13 -> x0, matrix products: 23.3 us -> none  [the longest x9 8.34 us: tap_sum(): jnp.dot(shifted, conv_weight[tap_idx * channels:(tap_idx + 1) * channels]...]
    ppermute x2 -> x0, waiting for transfers between devices: 11.4 us -> none  [the longest x1 7.35 us: extended(): lax.ppermute(lax.slice_in_dim(block, block.shape[dim] - width, None, axis...]
    all_to_all x1 -> x0, blocking collectives: 10.5 us -> none  [on_device(): lax.all_to_all(out_cols, 'lon', split_axis=1, concat_axis=2, tiled=True)]
    ppermute x2 -> x0, starting transfers between devices: 6.37 us -> none  [the longest x1 5.07 us: extended(): lax.ppermute(lax.slice_in_dim(block, block.shape[dim] - width, None, axis...]
    all_gather x1 -> x0, blocking collectives: 6.33 us -> none  [on_device(): bias_part = lax.all_gather(key_bias, 'lon', axis=1, tiled=True)]
    all_gather x2 -> x0, local copies, waits for them, and re-layouts: 5.19 us -> none  [the longest x1 2.6 us: on_device(): value_part = lax.all_gather(value_rows, 'lon', axis=1, tiled=True)]
  transfers between devices with their start and end apart: 5 -> 0, of which waited for: 5 -> 0; matrix products, arithmetic and copies ran while one was open for 6% -> 0% of each run, Pallas kernels for 0% -> 0%
where the time goes in v1:
time: 50.2 us; the launch traced here: 49.9 us
  Pallas kernels  42.7 us (85%)
  local copies, waits for them, and re-layouts  7.17 us (14%)
    pallas_call x1, Pallas kernels, fused(): pl.pallas_call(functools.partial(block_kernel, lat_count), out_shape=jax....  42.7 us
    unnamed x10, local copies, waits for them, and re-layouts  7.17 us

profile of v1, /device:TPU:0, one launch (start us, length us, event | category | flops | bytes accessed | tf_op | source)
XLA Modules:
  0.0 49.9 jit_solution(9668571027125301485)
XLA Ops:
  0.0 0.8 %copy.7.bias_ref = bf16[1,192,16]{2,1,0:T(8,128)(2,1)S(1)} copy(bf16[1,192,16]{1,2,0:T(8,128)(2,1)} %param.11) | data formatting | bytes 12288 | tf_op args[5]
  0.8 0.0 copy-start
  0.8 2.3 %copy-done = bf16[9216,256]{1,0:T(8,128)(2,1)S(1)} copy-done((bf16[9216,256]{1,0:T(8,128)(2,1)S(1)}, bf16[9216,256]{1,0:T(8,128)(2,1)}, u32[]{:S(2)}) %copy-start) | copy-done | bytes 4718616
  3.2 0.0 copy-start.1
  3.2 1.6 %copy-done.1 = bf16[1024,1024]{1,0:T(8,128)(2,1)S(1)} copy-done((bf16[1024,1024]{1,0:T(8,128)(2,1)S(1)}, bf16[1024,1024]{1,0:T(8,128)(2,1)}, u32[]{:S(2)}) %copy-start.1) | copy-done | bytes 2097176
  4.7 0.0 copy-start.2
  4.7 1.0 %copy-done.2 = bf16[1,192,1024]{2,1,0:T(8,128)(2,1)S(1)} copy-done((bf16[1,192,1024]{2,1,0:T(8,128)(2,1)S(1)}, bf16[1,192,1024]{2,1,0:T(8,128)(2,1)}, u32[]{:S(2)}) %copy-start.2) | copy-done | bytes 393240
  5.7 0.0 copy-start.3
  5.7 0.7 %copy-done.3 = f32[1024]{0:T(1024)S(1)} copy-done((f32[1024]{0:T(1024)S(1)}, f32[1024]{0:T(1024)}, u32[]{:S(2)}) %copy-start.3) | copy-done | bytes 4120
  6.4 42.7 %shard_map.64 = bf16[1,192,1024]{2,1,0:T(8,128)(2,1)S(1)} custom-call(bf16[1,192,1024]{2,1,0:T(8,128)(2,1)S(1)} %copy-done.2, bf16[9216,256]{1,0:T(8,128)(2,1)S(1)} %copy-done, f32[1,1024]{1,0:T(1,128)S(1)} %bitcast.1, bf16[1024,3072]{1,0:T(8,128)(2,1)} %qkv_ref.1, bf16[1024,1024]{1,0:T(8,128)(2,1)S(1)} %copy-done.1, bf16[1,192,16]{2,1,0:T(8,128)(2,1)S(1)} %copy.7.bias_ref), custom_call_target="tpu_custom_call" | custom-call | tf_op jit(solution)/shard_map/pallas_call | solution.py:424
  49.1 0.7 %copy.9 = bf16[1,192,1024]{2,1,0:T(8,128)(2,1)} copy(bf16[1,192,1024]{2,1,0:T(8,128)(2,1)S(1)} %shard_map.64) | data formatting | bytes 786432
Async XLA Ops:
  0.8 2.3 %copy-start = (bf16[9216,256]{1,0:T(8,128)(2,1)S(1)}, bf16[9216,256]{1,0:T(8,128)(2,1)}, u32[]{:S(2)}) copy-start(bf16[9216,256]{1,0:T(8,128)(2,1)} %conv_ref.1) | copy-start | bytes 14155780
  3.2 1.6 %copy-start.1 = (bf16[1024,1024]{1,0:T(8,128)(2,1)S(1)}, bf16[1024,1024]{1,0:T(8,128)(2,1)}, u32[]{:S(2)}) copy-start(bf16[1024,1024]{1,0:T(8,128)(2,1)} %outw_ref.1) | copy-start | bytes 6291460
  4.7 1.0 %copy-start.2 = (bf16[1,192,1024]{2,1,0:T(8,128)(2,1)S(1)}, bf16[1,192,1024]{2,1,0:T(8,128)(2,1)}, u32[]{:S(2)}) copy-start(bf16[1,192,1024]{2,1,0:T(8,128)(2,1)} %fields_ref.1) | copy-start | bytes 1179652
  5.7 0.7 %copy-start.3 = (f32[1024]{0:T(1024)S(1)}, f32[1024]{0:T(1024)}, u32[]{:S(2)}) copy-start(f32[1024]{0:T(1024)} %param.8) | copy-start | bytes 12292

commit v2 on v1

--- a/solution.py
+++ b/solution.py
@@ -104,11 +104,11 @@
 EDGE = 16
 PIECES = 2
 OWN_SIB, EDGE_P, EDGE_Q, BIAS_SIB, BIAS_P, BIAS_Q = 0, 1, 2, 3, 4, 5
-CONV_P, CONV_SIB, CONV_FWD = 6, 8, 10
-UP, DOWN = 12, 14
-ATT_P, ATT_Q, ATT_SIB = 16, 17, 18
-PIECE, PIECE_FWD = 19, 19 + PIECES
-COPIES = 19 + 2 * PIECES
+ATT_P, ATT_Q, ATT_SIB = 6, 7, 8
+UNITS = ((0, 0), (0, 1), (1, 0), (1, 1))
+CONV_P, CONV_SIB, CONV_FWD, UP, DOWN = 9, 13, 17, 21, 25
+PIECE, PIECE_FWD = 29, 29 + PIECES
+COPIES = 29 + 2 * PIECES
 
 
 def block_kernel(
@@ -124,14 +124,15 @@
     conv_w,
     qkv_w,
     out_w,
-    bias_own,
     bias_all,
+    bias_tile,
     part_send,
     part_recv,
     centre,
     cols,
     resid,
     normed,
+    mixed,
     proj,
     att_send,
     att,
@@ -190,14 +191,6 @@
     def _():
         pl.semaphore_signal(barrier, inc=1, device_id={"lat": row + 1}, device_id_type=MESH)
 
-    lane = lax.broadcasted_iota(jnp.int32, (H, 2 * head_dim), 1)
-    which = lax.broadcasted_iota(jnp.int32, (H, 2 * head_dim), 0)
-    spread = jnp.where((lane == which) | (lane == which + head_dim), 1.0, 0.0).astype(jnp.bfloat16)
-    bias_own[...] = jnp.dot(bias_ref[0], spread, preferred_element_type=jnp.float32).astype(
-        jnp.bfloat16
-    )
-    bias_all[rows_at(c * n, n)] = bias_own[...]
-
     pl.semaphore_wait(barrier, 3 + above.astype(jnp.int32) + below.astype(jnp.int32))
 
     sends = []
@@ -229,10 +222,11 @@
         for g in range(PIECES)
     ]
     biases = [
-        begin(remote(bias_own, bias_all.at[rows_at(c * n, n)], BIAS_SIB, {"lon": sib})),
-        begin(remote(bias_own, bias_all.at[rows_at(half + c * n, n)], BIAS_P, {"lon": p})),
-        begin(remote(bias_own, bias_all.at[rows_at(half + c * n, n)], BIAS_Q, {"lon": q})),
+        begin(remote(bias_ref, bias_all.at[c], BIAS_SIB, {"lon": sib})),
+        begin(remote(bias_ref, bias_all.at[2 + c], BIAS_P, {"lon": p})),
+        begin(remote(bias_ref, bias_all.at[2 + c], BIAS_Q, {"lon": q})),
     ]
+    bias_all[c] = bias_ref[...]
 
     def taps(k, a):
         full = EDGE + half + EDGE
@@ -249,47 +243,52 @@
             total = part if total is None else total + part
         return total[EDGE : EDGE + half]
 
-    up = [
-        remote(part_send.at[k, 0], part_recv.at[k, 0], UP + k, {"lat": row - 1}) for k in range(2)
-    ]
-    down = [
-        remote(part_send.at[k, 1], part_recv.at[k, 1], DOWN + k, {"lat": row + 1})
-        for k in range(2)
-    ]
-
-    def send_up(k):
-        part_send[k, 0] = taps(k, 2).astype(jnp.bfloat16)
-        pl.when(above)(up[k].start)
-
-    def send_down(k):
-        part_send[k, 1] = taps(k, 0).astype(jnp.bfloat16)
-        pl.when(below)(down[k].start)
-
-    conv_p = [
-        remote(cols.at[k, me], cols.at[1 - k, me], CONV_P + k, {"lon": p}) for k in range(2)
-    ]
-    conv_sib = [
-        remote(cols.at[k, me], cols.at[k, me], CONV_SIB + k, {"lon": sib}) for k in range(2)
-    ]
-    conv_fwd = [
-        remote(cols.at[1 - k, p], cols.at[1 - k, p], CONV_FWD + k, {"lon": sib})
-        for k in range(2)
-    ]
-
-    def finish_conv(k):
+    def unit_copies(first, make):
+        return {u: make(first + i, *u) for i, u in enumerate(UNITS)}
+
+    def part(k, side, h):
+        span = pl.ds(h * n, n)
+        return part_send.at[k, side, span], part_recv.at[k, side, span]
+
+    def block(k, o, h):
+        return cols.at[k, o, pl.ds(h * n, n)]
+
+    up = unit_copies(UP, lambda idx, k, h: remote(*part(k, 0, h), idx, {"lat": row - 1}))
+    down = unit_copies(DOWN, lambda idx, k, h: remote(*part(k, 1, h), idx, {"lat": row + 1}))
+    conv_p = unit_copies(
+        CONV_P, lambda idx, k, h: remote(block(k, me, h), block(1 - k, me, h), idx, {"lon": p})
+    )
+    conv_sib = unit_copies(
+        CONV_SIB, lambda idx, k, h: remote(block(k, me, h), block(k, me, h), idx, {"lon": sib})
+    )
+    conv_fwd = unit_copies(
+        CONV_FWD, lambda idx, k, h: remote(block(1 - k, p, h), block(1 - k, p, h), idx, {"lon": sib})
+    )
+
+    def send_part(k, side):
+        part_send[k, side] = taps(k, 0 if side else 2).astype(jnp.bfloat16)
+
+        @pl.when(below if side else above)
+        def _():
+            for h in range(2):
+                (down if side else up)[k, h].start()
+
+    def finish_conv(k, h):
+        span = slice(h * n, (h + 1) * n)
+
         @pl.when(below)
         def _():
-            up[k].wait_recv()
-            centre[k] = centre[k] + part_recv[k, 0].astype(jnp.float32)
+            up[k, h].wait_recv()
+            centre[k, span] = centre[k, span] + part_recv[k, 0, span].astype(jnp.float32)
 
         @pl.when(above)
         def _():
-            down[k].wait_recv()
-            centre[k] = centre[k] + part_recv[k, 1].astype(jnp.float32)
-
-        cols[k, me] = centre[k].astype(jnp.bfloat16)
-        begin(conv_p[k])
-        begin(conv_sib[k])
+            down[k, h].wait_recv()
+            centre[k, span] = centre[k, span] + part_recv[k, 1, span].astype(jnp.float32)
+
+        cols[k, me, span] = centre[k, span].astype(jnp.bfloat16)
+        begin(conv_p[k, h])
+        begin(conv_sib[k, h])
 
     loads[0].wait()
     to_sib.wait_recv()
@@ -298,62 +297,81 @@
     xbuf[1, 0:EDGE] = xbuf[0, half : half + EDGE]
     xbuf[1, EDGE + half : EDGE + half + EDGE] = xbuf[0, EDGE : EDGE + EDGE]
     loads[1].wait()
-    send_up(0)
+    send_part(0, 0)
     loads[2].wait()
-    send_down(0)
+    send_part(0, 1)
     loads[3].wait()
     centre[0] = taps(0, 1)
 
     forwards = []
-    for g in range(PIECES):
+
+    def pass_on(g):
         pieces[g].wait_recv()
         got = xbuf.at[1, rows_at(EDGE + c * n + g * piece, piece)]
         forwards.append(begin(remote(got, got, PIECE_FWD + g, {"lon": sib})))
-    finish_conv(0)
+
+    for g in range(PIECES - 1):
+        pass_on(g)
+    finish_conv(0, 0)
+    finish_conv(0, 1)
+    pass_on(PIECES - 1)
     for copy in forwards:
         copy.wait_recv()
-    send_up(1)
-    send_down(1)
+    send_part(1, 0)
+    send_part(1, 1)
     centre[1] = taps(1, 1)
-    conv_p[0].wait_recv()
-    begin(conv_fwd[0])
-    finish_conv(1)
+    finish_conv(1, 0)
+    finish_conv(1, 1)
+    for h in range(2):
+        conv_p[0, h].wait_recv()
+        begin(conv_fwd[0, h])
 
     for j in range(3):
         loads[4 + j].wait()
 
-    def project(k):
-        squares = jnp.zeros((half, 1), jnp.float32)
+    def project(k, h):
+        span = slice(h * n, (h + 1) * n)
+        squares = jnp.zeros((n, 1), jnp.float32)
         for o in range(blocks):
             lanes = slice(o * width, (o + 1) * width)
             summed = (
-                xbuf[k, EDGE : EDGE + half, lanes].astype(jnp.float32)
-                + cols[k, o].astype(jnp.float32)
+                xbuf[k, EDGE + h * n : EDGE + (h + 1) * n, lanes].astype(jnp.float32)
+                + cols[k, o, span].astype(jnp.float32)
             ).astype(jnp.bfloat16)
-            resid[k, :, lanes] = summed
+            resid[k, span, lanes] = summed
             wide = summed.astype(jnp.float32)
             squares = squares + jnp.sum(wide * wide, axis=-1, keepdims=True)
         scale = lax.rsqrt(squares / channels + 1e-06)
         for o in range(blocks):
             lanes = slice(o * width, (o + 1) * width)
             normed[:, lanes] = (
-                resid[k, :, lanes].astype(jnp.float32) * scale * gain_ref[:, lanes]
+                resid[k, span, lanes].astype(jnp.float32) * scale * gain_ref[:, lanes]
             ).astype(jnp.bfloat16)
         for j in range(3):
-            proj[j, k * half : (k + 1) * half] = jnp.dot(
+            proj[j, k * half + h * n : k * half + (h + 1) * n] = jnp.dot(
                 normed[...], qkv_w[j], preferred_element_type=jnp.float32
             ).astype(jnp.bfloat16)
 
-    conv_sib[1].wait_recv()
-    conv_fwd[0].wait_recv()
-    project(1)
-    conv_p[1].wait_recv()
-    begin(conv_fwd[1])
-    conv_sib[0].wait_recv()
-    conv_fwd[1].wait_recv()
-    project(0)
     for copy in biases:
         copy.wait_recv()
+    lane = lax.broadcasted_iota(jnp.int32, (H, 2 * head_dim), 1)
+    which = lax.broadcasted_iota(jnp.int32, (H, 2 * head_dim), 0)
+    spread = jnp.where((lane == which) | (lane == which + head_dim), 1.0, 0.0).astype(jnp.bfloat16)
+    for slot in range(4):
+        bias_tile[slot * n : (slot + 1) * n] = lax.dot_general(
+            bias_all[slot], spread, (((0,), (0,)), ((), ())), preferred_element_type=jnp.float32
+        ).astype(jnp.bfloat16)
+
+    for h in range(2):
+        conv_sib[1, h].wait_recv()
+        conv_fwd[0, h].wait_recv()
+        project(1, h)
+    for h in range(2):
+        conv_p[1, h].wait_recv()
+        begin(conv_fwd[1, h])
+        conv_sib[0, h].wait_recv()
+        conv_fwd[1, h].wait_recv()
+        project(0, h)
 
     tile = 2 * head_dim
     score_scale = 1.0 / math.sqrt(head_dim)
@@ -372,7 +390,7 @@
                 mine_k = (low_k >= head_dim) if odd else (low_k < head_dim)
                 picked = jnp.where(low_q == head + (0 if odd else head_dim), 1.0, 0.0)
                 q_ext = jnp.where(mine_q, queries, picked).astype(jnp.bfloat16)
-                k_ext = jnp.where(mine_k, keys, bias_all[...])
+                k_ext = jnp.where(mine_k, keys, bias_tile[...])
                 scores = lax.dot_general(
                     q_ext, k_ext, (((1,), (1,)), ((), ())), preferred_element_type=jnp.float32
                 )
@@ -392,23 +410,32 @@
     att_s = begin(remote(att_send.at[2], att.at[me], ATT_SIB, {"lon": sib}))
     attend(c * n, att.at[me])
     loads[7].wait()
-    for copy in (att_s, att_q, att_p):
-        copy.wait_recv()
-
-    for j in range(blocks):
-        lanes = slice(j * width, (j + 1) * width)
-        mixed = resid[0, rows_at(c * n, n), lanes].astype(jnp.float32)
-        for o in range(blocks):
-            mixed = mixed + jnp.dot(
-                att[o], out_w[o * width : (o + 1) * width, lanes], preferred_element_type=jnp.float32
+
+    def mix(o):
+        source = att[o]
+        for j in range(blocks):
+            lanes = slice(j * width, (j + 1) * width)
+            mixed[:, lanes] = mixed[:, lanes] + jnp.dot(
+                source,
+                out_w[pl.ds(pl.multiple_of(o * width, width), width), lanes],
+                preferred_element_type=jnp.float32,
             )
-        out_ref[0, :, lanes] = mixed.astype(jnp.bfloat16)
+
+    mixed[...] = resid[0, rows_at(c * n, n)].astype(jnp.float32)
+    mix(me)
+    att_s.wait_recv()
+    mix(sib)
+    att_q.wait_recv()
+    mix(q)
+    att_p.wait_recv()
+    mix(p)
+    out_ref[0] = mixed[...].astype(jnp.bfloat16)
 
     for copy in sends:
         copy.wait_send()
-    for k in range(2):
-        pl.when(above)(up[k].wait_send)
-        pl.when(below)(down[k].wait_send)
+    for u in UNITS:
+        pl.when(above)(up[u].wait_send)
+        pl.when(below)(down[u].wait_send)
 
 
 def fused(fields, conv_weight, norm_gain, qkv_weight, out_weight, key_bias):
@@ -431,14 +458,15 @@
             pltpu.VMEM(conv_weight.shape, bf16),
             pltpu.VMEM((3, channels, width), bf16),
             pltpu.VMEM(out_weight.shape, bf16),
-            pltpu.VMEM((n, 2 * head_dim), bf16),
+            pltpu.VMEM((4, H, n), bf16),
             pltpu.VMEM((2 * half, 2 * head_dim), bf16),
             pltpu.VMEM((2, 2, half, width), bf16),
             pltpu.VMEM((2, 2, half, width), bf16),
             pltpu.VMEM((2, half, width), f32),
             pltpu.VMEM((2, lon_count, half, width), bf16),
             pltpu.VMEM((2, half, channels), bf16),
-            pltpu.VMEM((half, channels), bf16),
+            pltpu.VMEM((n, channels), bf16),
+            pltpu.VMEM((n, channels), f32),
             pltpu.VMEM((3, 2 * half, width), bf16),
             pltpu.VMEM((3, n, width), bf16),
             pltpu.VMEM((lon_count, n, width), bf16),
@@ -447,9 +475,9 @@
             pltpu.SemaphoreType.DMA((8,)),
         ],
         compiler_params=pltpu.CompilerParams(
-            collective_id=0, has_side_effects=True, vmem_limit_bytes=44 * 1024 * 1024
+            collective_id=0, has_side_effects=True, vmem_limit_bytes=60 * 1024 * 1024
         ),
-    )(fields, conv_weight, norm_gain.reshape(1, channels), qkv_weight, out_weight, key_bias)
+    )(fields, conv_weight, norm_gain.reshape(1, channels), qkv_weight, out_weight, key_bias[0].T)
 
 
 def suits_kernel(fields, conv_weight):

time: 50.2 us -> 43.1 us (0.86)
  local copies, waits for them, and re-layouts: 7.17 us -> 1.77 us
  Pallas kernels: 42.7 us -> 41.1 us
    unnamed x10 -> x1, local copies, waits for them, and re-layouts: 7.17 us -> 1.77 us
    pallas_call x1, Pallas kernels: 42.7 us -> 41.1 us  [fused(): pl.pallas_call(functools.partial(block_kernel, lat_count), out_shape=jax....]
where the time goes in v2:
time: 43.1 us; the launch traced here: 42.8 us
  Pallas kernels  41.1 us (95%)
  local copies, waits for them, and re-layouts  1.77 us (4%)
    pallas_call x1, Pallas kernels, fused(): pl.pallas_call(functools.partial(block_kernel, lat_count), out_shape=jax....  41.1 us
    unnamed x1, local copies, waits for them, and re-layouts  1.77 us

profile of v2, /device:TPU:0, one launch (start us, length us, event | category | flops | bytes accessed | tf_op | source)
XLA Modules:
  0.0 42.8 jit_solution(6887503861110774907)
XLA Ops:
  0.0 41.1 %shard_map.64 = bf16[1,192,1024]{2,1,0:T(8,128)(2,1)} custom-call(bf16[1,192,1024]{2,1,0:T(8,128)(2,1)} %fields_ref.1, bf16[9216,256]{1,0:T(8,128)(2,1)} %conv_ref.1, f32[1,1024]{1,0:T(1,128)} %bitcast.5, bf16[1024,3072]{1,0:T(8,128)(2,1)} %qkv_ref.1, bf16[1024,1024]{1,0:T(8,128)(2,1)} %outw_ref.1, bf16[16,192]{1,0:T(8,128)(2,1)} %bitcast.4), custom_call_target="tpu_custom_call" | custom-call | tf_op jit(solution)/shard_map/pallas_call | solution.py:451
  41.1 1.8 %copy.8 = bf16[1,192,1024]{2,1,0:T(8,128)(2,1)} copy(bf16[1,192,1024]{2,1,0:T(8,128)(2,1)} %shard_map.64) | data formatting | bytes 786432
